TPU v7x, 32 devices: a whole 2x2x4 slice. The times are simulated.
32 devices in a mesh: grp: 2 (over y), col: 4 (over z), row: 2 (over x), dir: 2 (over core).
Axes of the slice: x: 2, y: 2, z: 4, core: 2. Of those that a mesh axis runs over, the one named last changes fastest.
Arguments:
- slopes_in: bfloat16 [512, 8192], P(None, ('grp', 'col')), parts along dimension 1, may hold values from -6 to 6
- basis_left: bfloat16 [12, 16, 256, 256], P(('row', 'dir'), 'col'), may hold values from -0.09375 to 0.09375
- basis_right: bfloat16 [12, 16, 256, 256], P(('row', 'dir'), 'col'), may hold values from -0.375 to 0.375
- rank_blocks: int32 [12, 16], P(('row', 'dir'), 'col'), may hold values from 1 to 4
- tile_owner: int32 [16], replicated, may hold values from 0 to 15, each once
- footprint: int32 [4, 4, 4, 2048], P(('row', 'dir')), may hold values from 0 to 767
- trace_weight: float32 [4, 4, 4, 2048], P(('row', 'dir')), may hold values from 0 to 0.5
- fitting: bfloat16 [2048, 4096], P(None, 'col'), may hold values from -0.125 to 0.125
Outputs:
- commands: bfloat16 [4, 1024, 4096], P(('row', 'dir'), 'grp', 'col'), parts along dimension 1
There are 2 independent parts, one for each index of `grp`. A program takes and returns all parts, laid end to end along the dimension named above; an argument that names none is the same for every part. Nothing has to cross between parts.
Inputs may be any that keep to these rules, and one draw needn't show every extreme that they name: rank_blocks[i, k] is the number of leading blocks of 64 columns of tile (i, k) that are live. `tile_owner`: each slope block appears in exactly one tile slot. `footprint`: indices into one layer's points.
All inputs are finite; a program needn't handle non-finite values.
Results may differ from a plain program's by a relative error of at most 0.0064.
Values may be sent and summed in bfloat16 or wider, within the bound.
A program may use at most 128 MiB of HBM per device.

v0:
```python
import jax
import jax.numpy as jnp
from jax import lax
from jax.sharding import PartitionSpec as P

RB = 64


def shards(
    slopes_in, basis_left, basis_right, rank_blocks, tile_owner, footprint, trace_weight, fitting
):
    frames = slopes_in.shape[0]
    tile_size = basis_left.shape[2]
    rows_here = basis_left.shape[0]
    slots_here = basis_left.shape[1]
    rank_cols = basis_left.shape[3]
    owners = lax.dynamic_slice_in_dim(tile_owner, lax.axis_index("col") * slots_here, slots_here, 0)
    share = frames // lax.axis_size(("row", "dir"))
    mine = lax.dynamic_slice_in_dim(slopes_in, lax.axis_index(("row", "dir")) * share, share, 0)
    partial_value = lax.all_gather(mine, "col", axis=1, tiled=True)
    picked = jnp.take(partial_value.reshape(share, -1, tile_size), owners, axis=1)
    chosen = lax.all_gather(picked, ("row", "dir"), axis=0, tiled=True)
    columns = jnp.arange(rank_cols, dtype=jnp.int32) // RB
    live = columns[None, None, None, :] < rank_blocks[:, :, None, None]
    frame_share = frames // lax.axis_size("col")
    coeffs = jnp.einsum("fkn,iknr->ikfr", chosen, basis_right, preferred_element_type=jnp.float32)
    coeffs = jnp.where(live, coeffs, 0.0).astype(jnp.bfloat16)
    summed = jnp.einsum("ikfr,iknr->fin", coeffs, basis_left, preferred_element_type=jnp.float32)
    layer_block = lax.psum_scatter(
        summed.reshape(lax.axis_size("col") * frame_share, rows_here * tile_size),
        "col",
        scatter_dimension=0,
        tiled=True,
    ).astype(jnp.bfloat16)
    layers = lax.all_gather(layer_block, ("row", "dir"), axis=1, tiled=True)
    layer_count = footprint.shape[1]
    pupil_count = footprint.shape[3]
    per_layer = layers.shape[1] // layer_count
    shifts = (jnp.arange(layer_count, dtype=jnp.int32) * per_layer)[:, None, None]
    flat = (footprint[0] + shifts).reshape(-1)
    values = (
        jnp.take(layers, flat, axis=1)
        .astype(jnp.float32)
        .reshape(frame_share, layer_count, 4, pupil_count)
    )
    pupil = jnp.sum(values * trace_weight[0][None], axis=(1, 2)).astype(jnp.bfloat16)
    commands = jnp.dot(
        lax.all_gather(pupil, "col", axis=0, tiled=True),
        fitting,
        preferred_element_type=jnp.float32,
    )
    return commands.astype(jnp.bfloat16)[None]


def solution(mesh):
    placed = (
        P(None, ("grp", "col")),
        P(("row", "dir"), "col", None, None),
        P(("row", "dir"), "col", None, None),
        P(("row", "dir"), "col"),
        P(),
        P(("row", "dir"), None, None, None),
        P(("row", "dir"), None, None, None),
        P(None, "col"),
    )
    return jax.shard_map(
        shards,
        mesh=mesh,
        in_specs=placed,
        out_specs=P(("row", "dir"), "grp", "col"),
        check_vma=False,
    )
```

profile of v0, /device:TPU:0, one launch (start us, length us, event | category | flops | bytes accessed | tf_op | source)
XLA Modules:
  0.0 294.1 jit_solution(6185712206535708235)
XLA Ops:
  6.5 0.0 copy-start
  6.5 0.0 copy-start.1
  6.5 0.0 copy-start.3
  6.5 0.0 all-gather.4.cloned.1.call-start
  6.6 1.1 constant_dynamic-slice_fusion
  7.7 0.8 copy.14
  8.5 0.0 all-gather.4.cloned.1.call-update
  8.5 0.0 all-gather.6.cloned.1.call-start
  8.6 0.7 compare_and_fusion.1
  9.3 30.3 %all-gather.4.cloned.1.call-done = bf16[128,4096]{0,1:T(8,128)(2,1)} async-done(((bf16[128,1024]{0,1:T(8,128)(2,1)}), bf16[128,4096]{0,1:T(8,128)(2,1)}) %all-gather.4.cloned.1.call-update) | async-done | bytes 1048592 | tf_op jit(solution)/shard_map/all_gather | solution.py:20
  39.6 1.5 copy.12
  41.1 0.6 gather_fusion
  41.7 0.8 select_bitcast_fusion
  42.5 0.0 all-gather.6.cloned.1.call-update
  42.5 0.0 reduce-scatter.2.cloned.1.call-start
  42.5 0.1 add.67
  42.6 0.2 add.75
  42.8 0.0 copy-done.1
  42.8 0.2 squeeze.6
  43.0 0.0 copy-done.3
  43.0 0.1 broadcast_compare_fusion
  43.1 15.8 %all-gather.6.cloned.1.call-done = bf16[512,4,256]{2,0,1:T(8,128)(2,1)} async-done(((bf16[128,4,256]{2,0,1:T(8,128)(2,1)}), bf16[512,4,256]{2,0,1:T(8,128)(2,1)}) %all-gather.6.cloned.1.call-update) | async-done | bytes 1048592 | tf_op jit(solution)/shard_map/all_gather | solution.py:22
  58.8 0.0 copy-done
  58.8 4.7 %fusion.1 = f32[3,512,256,1]{1,2,3,0:T(8,128)} fusion(bf16[3,4,256,256]{3,2,1,0:T(8,128)(2,1)S(1)} %copy-done, pred[3,4,256]{2,1,0:T(4,128)(4,1)S(1)} %broadcast_compare_fusion, bf16[3,4,256,256]{3,2,1,0:T(8,128)(2,1)} %param.10, bf16[512,4,256]{2,0,1:T(8,128)(2,1)} %all-gather.6.cloned.1.call-done), kind=kOutput, calls=%fused_computation.5 | convolution fusion | flops 1613758464 | bytes 5770240 | tf_op jit(solution)/shard_map/ikfr,iknr->fin/dot_general | solution.py:28
  63.5 0.0 reduce-scatter.2.cloned.1.call-update
  63.6 0.0 all-gather.8.cloned.1.call-start
  63.6 0.2 compare_select_fusion
  63.8 0.2 compare_and_fusion
  64.0 35.0 %reduce-scatter.2.cloned.1.call-done = f32[128,768]{0,1:T(8,128)} async-done(((f32[512,768]{0,1:T(8,128)}), f32[128,768]{0,1:T(8,128)}) %reduce-scatter.2.cloned.1.call-update) | async-done | bytes 393232 | tf_op jit(solution)/shard_map/reduce_scatter | solution.py:29
  99.0 1.0 convert_element_type.17
  100.0 8.6 %all_gather.14 = bf16[128,3072]{0,1:T(8,128)(2,1)S(1)} all-gather(bf16[128,768]{0,1:T(8,128)(2,1)S(1)} %convert_element_type.17), channel_id=1, replica_groups=mesh['grp'=2,'col'=4,'row'=2,'dir'=2] {'row','dir'}, dimensions={1}, use_global_device_ids=true | all-gather | bytes 983040 | tf_op jit(solution)/shard_map/all_gather | solution.py:35
  108.6 0.0 copy-start.2
  108.6 114.3 %gather_fusion.1 = bf16[32768,128]{1,0:T(8,128)(2,1)} fusion(bf16[128,3072]{0,1:T(8,128)(2,1)S(1)} %all_gather.14, s32[32768]{0:T(1024)S(1)} %broadcast_clamp_fusion), kind=kCustom, calls=%fused_computation.1 | custom fusion | bytes 16908288 | tf_op jit(solution)/shard_map/jit(_take)/gather | solution.py:42
  222.9 0.0 copy-done.2
  222.9 13.4 %multiply_reduce_fusion = bf16[128,2048]{0,1:T(8,128)(2,1)} fusion(f32[4,4,2048]{2,1,0:T(4,128)S(1)} %bitcast.39, bf16[128,4,4,2048]{0,3,2,1:T(8,128)(2,1)} %bitcast.35, pred[4,4,2048]{2,1,0:T(4,128)(4,1)S(1)} %compare_and_fusion), kind=kLoop, calls=%fused_computation.2 | loop fusion | flops 16515072 | bytes 9076736 | tf_op jit(solution)/shard_map/reduce_sum | solution.py:46
  236.3 0.0 all-gather.8.cloned.1.call-update
  236.3 45.1 %all-gather.8.cloned.1.call-done = bf16[512,2048]{0,1:T(8,128)(2,1)} async-done(((bf16[128,2048]{0,1:T(8,128)(2,1)}), bf16[512,2048]{0,1:T(8,128)(2,1)}) %all-gather.8.cloned.1.call-update) | async-done | bytes 2097168 | tf_op jit(solution)/shard_map/all_gather | solution.py:48
  281.4 6.1 %fusion.7 = bf16[1,512,1024]{2,1,0:T(8,128)(2,1)} fusion(bf16[512,2048]{0,1:T(8,128)(2,1)} %all-gather.8.cloned.1.call-done, bf16[2048,1024]{1,0:T(8,128)(2,1)} %param.15), kind=kOutput, calls=%fused_computation.10 | convolution fusion | flops 2148007936 | bytes 7340032 | tf_op jit(solution)/shard_map/dot_general | solution.py:47
  (4 shorter events, 0.0 us)
Async XLA Ops:
  6.5 52.3 %copy-start = (bf16[3,4,256,256]{3,2,1,0:T(8,128)(2,1)S(1)}, bf16[3,4,256,256]{3,2,1,0:T(8,128)(2,1)}, u32[]{:S(2)}) copy-start(bf16[3,4,256,256]{3,2,1,0:T(8,128)(2,1)} %param.9) | copy-start | bytes 4718596
  6.5 36.3 %copy-start.1 = (s32[1,4,4,2048]{3,2,1,0:T(4,128)S(1)}, s32[1,4,4,2048]{3,2,1,0:T(4,128)}, u32[]{:S(2)}) copy-start(s32[1,4,4,2048]{3,2,1,0:T(4,128)} %param.13) | copy-start | bytes 393220
  6.5 36.5 %copy-start.3 = (s32[3,4]{1,0:T(4,128)S(1)}, s32[3,4]{1,0:T(4,128)}, u32[]{:S(2)}) copy-start(s32[3,4]{1,0:T(4,128)} %param.11) | copy-start | bytes 148
  6.5 33.1 %all-gather.4.cloned.1.call-start = ((), (), s32[]{:S(2)}) async-start(), calls=%async_computation.1 | async-start | bytes 1310720 | tf_op jit(solution)/shard_map/all_gather | solution.py:20
  8.5 50.3 %all-gather.6.cloned.1.call-start = ((), (), s32[]{:S(2)}) async-start(), calls=%async_computation.2 | async-start | bytes 1310720 | tf_op jit(solution)/shard_map/all_gather | solution.py:22
  42.5 56.5 %reduce-scatter.2.cloned.1.call-start = ((), (), s32[]{:S(2)}) async-start(), calls=%async_computation.3 | async-start | bytes 1966080 | tf_op jit(solution)/shard_map/reduce_scatter | solution.py:29
  63.6 217.8 %all-gather.8.cloned.1.call-start = ((), (), s32[]{:S(2)}) async-start(), calls=%async_computation.4 | async-start | bytes 2621440 | tf_op jit(solution)/shard_map/all_gather | solution.py:48
  108.6 114.3 %copy-start.2 = (f32[1,4,4,2048]{3,2,1,0:T(4,128)S(1)}, f32[1,4,4,2048]{3,2,1,0:T(4,128)}, u32[]{:S(2)}) copy-start(f32[1,4,4,2048]{3,2,1,0:T(4,128)} %param.14) | copy-start | bytes 393220
Sparse Core Ops, SparseCore 0:
  8.9 30.6 all-gather.3
  42.6 16.2 all-gather.5
  63.7 35.2 reduce-scatter.1
  236.4 44.9 all-gather.7
where the time goes:
time: 294 us
  waiting for transfers between devices  126 us (43%)
  local copies, waits for them, and re-layouts  119 us (40%)
  other arithmetic  16.4 us (6%)
  between operations  13.2 us (4%)
  matrix products  10.8 us (4%)
  blocking collectives  8.57 us (3%)
    gather x1, local copies, waits for them, and re-layouts, shards(): jnp.take(layers, flat, axis=1).astype(jnp.float32)  114 us
    all_gather x1, waiting for transfers between devices, shards(): lax.all_gather(pupil, 'col', axis=0, tiled=True)  45.1 us
    reduce_scatter x1, waiting for transfers between devices, shards(): lax.psum_scatter(summed.reshape(lax.axis_size('col') * frame_share, rows_...  35 us
    all_gather x1, waiting for transfers between devices, shards(): partial_value = lax.all_gather(mine, 'col', axis=1, tiled=True)  30.3 us
    all_gather x1, waiting for transfers between devices, shards(): chosen = lax.all_gather(picked, ('row', 'dir'), axis=0, tiled=True)  15.8 us
    reduce_sum x1, other arithmetic, shards(): jnp.sum(values * trace_weight[0][None], axis=(1, 2)).astype(jnp.bfloat16)  13.4 us
    all_gather x1, blocking collectives, shards(): layers = lax.all_gather(layer_block, ('row', 'dir'), axis=1, tiled=True)  8.57 us
    dot_general x1, matrix products, shards(): jnp.dot(lax.all_gather(pupil, 'col', axis=0, tiled=True), fitting, prefer...  6.14 us
  transfers between devices with their start and end apart: 4, of which 4 were waited for; matrix products, arithmetic and copies ran while one was open for 1% of the time, Pallas kernels for 0%

commit v1 on v0

v1 whole, which is shorter than its diff:
```python
import functools

import jax
import jax.numpy as jnp
from jax import lax
from jax.experimental import pallas as pl
from jax.experimental.pallas import tpu as pltpu
from jax.sharding import PartitionSpec as P

RB = 64
MESH = pl.DeviceIdType.MESH


def plain(
    slopes_in, basis_left, basis_right, rank_blocks, tile_owner, footprint, trace_weight, fitting
):
    frames = slopes_in.shape[0]
    tile_size = basis_left.shape[2]
    rows_here, slots_here = basis_left.shape[:2]
    rank_cols = basis_left.shape[3]
    owners = lax.dynamic_slice_in_dim(tile_owner, lax.axis_index("col") * slots_here, slots_here, 0)
    share = frames // lax.axis_size(("row", "dir"))
    mine = lax.dynamic_slice_in_dim(slopes_in, lax.axis_index(("row", "dir")) * share, share, 0)
    gathered = lax.all_gather(mine, "col", axis=1, tiled=True)
    picked = jnp.concatenate(
        [
            lax.dynamic_slice_in_dim(gathered, owners[k] * tile_size, tile_size, 1)
            for k in range(slots_here)
        ],
        axis=1,
    )
    chosen = lax.all_gather(picked, ("row", "dir"), axis=0, tiled=True)
    chosen = chosen.reshape(frames, slots_here, tile_size)
    columns = jnp.arange(rank_cols, dtype=jnp.int32) // RB
    live = columns[None, None, None, :] < rank_blocks[:, :, None, None]
    coeffs = jnp.einsum("fkn,iknr->ikfr", chosen, basis_right, preferred_element_type=jnp.float32)
    coeffs = jnp.where(live, coeffs, 0.0).astype(jnp.bfloat16)
    summed = jnp.einsum("ikfr,iknr->fin", coeffs, basis_left, preferred_element_type=jnp.float32)
    layer_block = lax.psum_scatter(
        summed.reshape(frames, rows_here * tile_size), "col", scatter_dimension=0, tiled=True
    ).astype(jnp.bfloat16)
    layers = lax.all_gather(layer_block, ("row", "dir"), axis=1, tiled=True)
    layer_count, taps, pupil_count = footprint.shape[1:]
    per_layer = layers.shape[1] // layer_count
    points = jnp.arange(per_layer, dtype=jnp.int32)[:, None]
    total = 0.0
    for l in range(layer_count):
        spread = 0.0
        for t in range(taps):
            spread += jnp.where(
                points == footprint[0, l, t][None, :], trace_weight[0, l, t][None, :], 0.0
            )
        total += jnp.dot(
            layers[:, l * per_layer : (l + 1) * per_layer],
            spread.astype(jnp.bfloat16),
            preferred_element_type=jnp.float32,
        )
    commands = jnp.dot(
        lax.all_gather(total.astype(jnp.bfloat16), "col", axis=0, tiled=True),
        fitting,
        preferred_element_type=jnp.float32,
    )
    return commands.astype(jnp.bfloat16)[None]


def fused_kernel(
    nc,
    owner_ref,
    ranks_ref,
    slopes_hbm,
    left_hbm,
    right_hbm,
    foot_ref,
    weight_ref,
    fit_hbm,
    out_ref,
    left,
    right,
    fit,
    parts,
    picks,
    chosen,
    spread,
    mixing,
    partial_sums,
    arrived,
    layers,
    load_sem,
    a1_send,
    a1_recv,
    a2_send,
    a2_recv,
    a3x_send,
    a3x_recv,
    a3c_send,
    a3c_recv,
    rs_send,
    rs_recv,
    z_send,
    z_recv,
    x_send,
    x_recv,
    c_send,
    c_recv,
):
    rows_here, slots, tile, rank_cols = left.shape
    frames = slopes_hbm.shape[0]
    quads = chosen.shape[0]
    share = frames // quads
    pieces = quads // nc
    block = frames // nc
    col, row, core = lax.axis_index("col"), lax.axis_index("row"), lax.axis_index("dir")
    here = row * 2 + core
    beside = (1 - row) * 2 + core
    sibling = {"dir": 1 - core}
    across = {"row": 1 - row}

    def ahead(j):
        return lax.rem(col + j, nc)

    def behind(j):
        return lax.rem(col + nc - j, nc)

    loads = [
        pltpu.make_async_copy(right_hbm, right, load_sem.at[0]),
        pltpu.make_async_copy(left_hbm, left, load_sem.at[1]),
        pltpu.make_async_copy(fit_hbm, fit, load_sem.at[2]),
    ]

    barrier = pltpu.get_barrier_semaphore()
    for j in range(1, nc):
        pl.semaphore_signal(barrier, inc=1, device_id={"col": ahead(j)}, device_id_type=MESH)
    for other in (sibling, across):
        pl.semaphore_signal(barrier, inc=1, device_id=other, device_id_type=MESH)
    pl.semaphore_wait(barrier, nc + 1)

    def remote(src, dst, send, recv, target):
        return pltpu.make_async_remote_copy(
            src_ref=src,
            dst_ref=dst,
            send_sem=send,
            recv_sem=recv,
            device_id=target,
            device_id_type=MESH,
        )

    sent = []
    for j in range(1, nc):
        start = pl.multiple_of((ahead(j) * pieces + here) * share, share)
        for b in range(slots):
            copy = remote(
                slopes_hbm.at[pl.ds(start, share), pl.ds(b * tile, tile)],
                parts.at[col * slots + b],
                a1_send.at[(j - 1) * slots + b],
                a1_recv.at[(j - 1) * slots + b],
                {"col": ahead(j)},
            )
            copy.start()
            sent.append(copy)
    first = sent
    start = pl.multiple_of((col * pieces + here) * share, share)
    own = []
    for b in range(slots):
        copy = pltpu.make_async_copy(
            slopes_hbm.at[pl.ds(start, share), pl.ds(b * tile, tile)],
            parts.at[col * slots + b],
            load_sem.at[3 + b],
        )
        copy.start()
        own.append(copy)
    for copy in loads:
        copy.start()
    loads[2].wait()

    layer_count, taps, pupil_count = foot_ref.shape[1:]
    points = mixing.shape[0]
    per_layer = points // layer_count
    step = spread.shape[0]
    per_step = per_layer // step
    steps = points // step
    wide = 256

    def mix(n, carry):
        l, base = n // per_step, (n % per_step) * step
        at = lax.broadcasted_iota(jnp.int32, (step, wide), 0) + base
        for m in range(0, pupil_count, wide):
            total = jnp.zeros((step, wide), jnp.float32)
            for t in range(taps):
                total += jnp.where(
                    at == foot_ref[0, l, t : t + 1, m : m + wide],
                    weight_ref[0, l, t : t + 1, m : m + wide],
                    0.0,
                )
            spread[:, m : m + wide] = total.astype(jnp.bfloat16)
        mixing[pl.ds(pl.multiple_of(n * step, step), step), :] = jnp.dot(
            spread[...], fit[...], preferred_element_type=jnp.float32
        ).astype(jnp.bfloat16)
        return carry

    cuts = [0, steps // 4, steps // 2, steps]
    lax.fori_loop(cuts[0], cuts[1], mix, 0)

    for copy in own:
        copy.wait()
    for copy in first:
        copy.wait_recv()
    second = []
    for j in range(nc):
        for k in range(slots):
            picks[ahead(j), k] = parts[owner_ref[ahead(j) * slots + k]]
        if j:
            copy = remote(
                picks.at[ahead(j)],
                chosen.at[col * pieces + here],
                a2_send.at[j - 1],
                a2_recv.at[j - 1],
                {"col": ahead(j)},
            )
            copy.start()
            second.append(copy)
    chosen[col * pieces + here] = picks[col]

    third = []

    def spread_share(j):
        at = behind(j) * pieces + here
        for send, recv, target in (
            (a3x_send.at[j], a3x_recv.at[j], across),
            (a3c_send.at[j], a3c_recv.at[j], sibling),
        ):
            copy = remote(chosen.at[at], chosen.at[at], send, recv, target)
            copy.start()
            third.append(copy)

    spread_share(0)
    lax.fori_loop(cuts[1], cuts[2], mix, 0)
    for j in range(1, nc):
        second[j - 1].wait_recv()
        spread_share(j)
    fourth = []
    for j in range(nc):
        third[2 * j].wait_recv()
        at = behind(j) * pieces + beside
        copy = remote(
            chosen.at[at], chosen.at[at], a3c_send.at[nc + j], a3c_recv.at[nc + j], sibling
        )
        copy.start()
        fourth.append(copy)
    for j in range(nc):
        third[2 * j + 1].wait_recv()
        fourth[j].wait_recv()
    loads[0].wait()
    loads[1].wait()

    lane = lax.broadcasted_iota(jnp.int32, (1, rank_cols), 1)
    sums = []
    for i in range(rows_here):
        total = jnp.zeros((frames, tile), jnp.float32)
        for k in range(slots):
            coeffs = jnp.dot(
                chosen[:, k].reshape(frames, tile), right[i, k], preferred_element_type=jnp.float32
            )
            coeffs = jnp.where(lane < ranks_ref[i, k] * RB, coeffs, 0.0).astype(jnp.bfloat16)
            total += lax.dot_general(
                coeffs, left[i, k], (((1,), (1,)), ((), ())), preferred_element_type=jnp.float32
            )
        partial_sums[i] = total.astype(jnp.bfloat16).reshape(nc, block, tile)
        for j in range(1, nc):
            copy = remote(
                partial_sums.at[i, ahead(j)],
                arrived.at[j - 1, i],
                rs_send.at[(j - 1) * rows_here + i],
                rs_recv.at[(j - 1) * rows_here + i],
                {"col": ahead(j)},
            )
            copy.start()
            sums.append(copy)
    lax.fori_loop(cuts[2], cuts[3], mix, 0)
    for copy in sums:
        copy.wait_recv()
    for i in range(rows_here):
        total = partial_sums[i, col].astype(jnp.float32)
        for j in range(1, nc):
            total += arrived[j - 1, i].astype(jnp.float32)
        layers[here, col, :, i * tile : (i + 1) * tile] = total.astype(jnp.bfloat16)

    along = []
    for j in range(1, nc):
        at = layers.at[here, col]
        copy = remote(at, at, z_send.at[j - 1], z_recv.at[j - 1], {"col": ahead(j)})
        copy.start()
        along.append(copy)
    over, within = [], []

    def spread_layers(j):
        at = layers.at[here, behind(j)]
        copy = remote(at, at, x_send.at[j], x_recv.at[j], across)
        copy.start()
        over.append(copy)
        copy = remote(at, at, c_send.at[j], c_recv.at[j], sibling)
        copy.start()
        within.append(copy)

    spread_layers(0)
    for j in range(1, nc):
        along[j - 1].wait_recv()
        spread_layers(j)
    passed = []
    for j in range(nc):
        over[j].wait_recv()
        at = layers.at[beside, behind(j)]
        copy = remote(at, at, c_send.at[nc + j], c_recv.at[nc + j], sibling)
        copy.start()
        passed.append(copy)
    for j in range(nc):
        within[j].wait_recv()
        passed[j].wait_recv()
    depth = layers.shape[3]
    total = jnp.zeros(out_ref.shape[1:], jnp.float32)
    for r in range(pieces):
        total += jnp.dot(
            layers[r].reshape(frames, depth),
            mixing[r * depth : (r + 1) * depth, :],
            preferred_element_type=jnp.float32,
        )
    out_ref[0] = total.astype(jnp.bfloat16)
    for copy in first + second + third + fourth + sums + along + over + within + passed:
        copy.wait_send()


def fused(
    nc, slopes_in, basis_left, basis_right, rank_blocks, tile_owner, footprint, trace_weight, fitting
):
    frames = slopes_in.shape[0]
    rows_here, slots, tile, rank_cols = basis_left.shape
    pieces = 4
    share = frames // (nc * pieces)
    points = rows_here * tile * pieces
    pupil_count, acts = fitting.shape
    step = tile
    bf16 = jnp.bfloat16
    dma = pltpu.SemaphoreType.DMA
    anywhere = pl.BlockSpec(memory_space=pl.ANY)
    smem = pl.BlockSpec(memory_space=pltpu.SMEM)
    vmem = pl.BlockSpec(memory_space=pltpu.VMEM)
    return pl.pallas_call(
        functools.partial(fused_kernel, nc),
        out_shape=jax.ShapeDtypeStruct((1, frames, acts), bf16),
        in_specs=[smem, smem, anywhere, anywhere, anywhere, vmem, vmem, anywhere],
        out_specs=vmem,
        scratch_shapes=[
            pltpu.VMEM(basis_left.shape, bf16),
            pltpu.VMEM(basis_right.shape, bf16),
            pltpu.VMEM(fitting.shape, bf16),
            pltpu.VMEM((nc * slots, share, tile), bf16),
            pltpu.VMEM((nc, slots, share, tile), bf16),
            pltpu.VMEM((nc * pieces, slots, share, tile), bf16),
            pltpu.VMEM((step, pupil_count), bf16),
            pltpu.VMEM((points, acts), bf16),
            pltpu.VMEM((rows_here, nc, frames // nc, tile), bf16),
            pltpu.VMEM((nc - 1, rows_here, frames // nc, tile), bf16),
            pltpu.VMEM((pieces, nc, frames // nc, rows_here * tile), bf16),
            dma((3 + slots,)),
            dma(((nc - 1) * slots,)),
            dma(((nc - 1) * slots,)),
            dma((nc - 1,)),
            dma((nc - 1,)),
            dma((nc,)),
            dma((nc,)),
            dma((2 * nc,)),
            dma((2 * nc,)),
            dma(((nc - 1) * rows_here,)),
            dma(((nc - 1) * rows_here,)),
            dma((nc - 1,)),
            dma((nc - 1,)),
            dma((nc,)),
            dma((nc,)),
            dma((2 * nc,)),
            dma((2 * nc,)),
        ],
        compiler_params=pltpu.CompilerParams(
            collective_id=0, has_side_effects=True, vmem_limit_bytes=52 * 2**20
        ),
    )(
        tile_owner,
        rank_blocks,
        slopes_in,
        basis_left,
        basis_right,
        footprint,
        trace_weight,
        fitting,
    )


def solution(mesh):
    placed = (
        P(None, ("grp", "col")),
        P(("row", "dir"), "col", None, None),
        P(("row", "dir"), "col", None, None),
        P(("row", "dir"), "col"),
        P(),
        P(("row", "dir"), None, None, None),
        P(("row", "dir"), None, None, None),
        P(None, "col"),
    )

    def shards(slopes_in, basis_left, basis_right, rank_blocks, tile_owner, footprint, *rest):
        nc = mesh.shape["col"]
        pieces = mesh.shape["row"] * mesh.shape["dir"]
        tile = basis_left.shape[2]
        per_layer = basis_left.shape[0] * pieces * tile // footprint.shape[1]
        fits = (
            mesh.shape["row"] == 2
            and mesh.shape["dir"] == 2
            and nc > 1
            and slopes_in.shape[0] % (nc * pieces * 16) == 0
            and slopes_in.shape[1] == basis_left.shape[1] * tile
            and per_layer % tile == 0
        )
        body = functools.partial(fused, nc) if fits else plain
        return body(
            slopes_in, basis_left, basis_right, rank_blocks, tile_owner, footprint, *rest
        )

    return jax.shard_map(
        shards,
        mesh=mesh,
        in_specs=placed,
        out_specs=P(("row", "dir"), "grp", "col"),
        check_vma=False,
    )
```

time: 294 us -> 79.8 us (0.27)
  the two profiles are of different devices: /device:TPU:0 before, /device:TPU:27 now
where the time goes in v1:
time: 79.8 us; the launch traced here: 79.6 us
  Pallas kernels  75.5 us (95%)
  local copies, waits for them, and re-layouts  4.12 us (5%)
    pallas_call x1, Pallas kernels, fused(): pl.pallas_call(functools.partial(fused_kernel, nc), out_shape=jax.ShapeDt...  75.5 us
    unnamed x9, local copies, waits for them, and re-layouts  4.12 us

profile of v1, /device:TPU:27, one launch (start us, length us, event | category | flops | bytes accessed | tf_op | source)
XLA Modules:
  0.0 79.6 jit_solution(17066620019041861674)
XLA Ops:
  0.0 0.0 copy-start
  0.0 0.9 %copy-done = s32[1,4,4,2048]{3,2,1,0:T(4,128)S(1)} copy-done((s32[1,4,4,2048]{3,2,1,0:T(4,128)S(1)}, s32[1,4,4,2048]{3,2,1,0:T(4,128)}, u32[]{:S(2)}) %copy-start) | copy-done | bytes 131096
  0.9 0.0 copy-start.1
  0.9 0.9 %copy-done.1 = f32[1,4,4,2048]{3,2,1,0:T(4,128)S(1)} copy-done((f32[1,4,4,2048]{3,2,1,0:T(4,128)S(1)}, f32[1,4,4,2048]{3,2,1,0:T(4,128)}, u32[]{:S(2)}) %copy-start.1) | copy-done | bytes 131096
  1.8 0.0 copy-start.2
  1.8 0.7 copy-done.2
  2.5 0.0 copy-start.3
  2.5 0.7 copy-done.3
  3.1 75.5 %shard_map.82 = bf16[1,512,1024]{2,1,0:T(8,128)(2,1)S(1)} custom-call(s32[16]{0:T(128)S(1)} %copy-done.3, s32[3,4]{1,0:T(4,128)S(1)} %copy-done.2, bf16[512,1024]{1,0:T(8,128)(2,1)} %slopes_hbm.1, bf16[3,4,256,256]{3,2,1,0:T(8,128)(2,1)} %left_hbm.1, bf16[3,4,256,256]{3,2,1,0:T(8,128)(2,1)} %right_hbm.1, s32[1,4,4,2048]{3,2,1,0:T(4,128)S(1)} %copy-done, ...), custom_call_target="tpu_custom_call" | custom-call | tf_op jit(solution)/shard_map/pallas_call | solution.py:346
  78.7 1.0 %copy.10 = bf16[1,512,1024]{2,1,0:T(8,128)(2,1)} copy(bf16[1,512,1024]{2,1,0:T(8,128)(2,1)S(1)} %shard_map.82) | data formatting | bytes 2097152
Async XLA Ops:
  0.0 0.9 %copy-start = (s32[1,4,4,2048]{3,2,1,0:T(4,128)S(1)}, s32[1,4,4,2048]{3,2,1,0:T(4,128)}, u32[]{:S(2)}) copy-start(s32[1,4,4,2048]{3,2,1,0:T(4,128)} %foot_ref.1) | copy-start | bytes 393220
  0.9 0.9 %copy-start.1 = (f32[1,4,4,2048]{3,2,1,0:T(4,128)S(1)}, f32[1,4,4,2048]{3,2,1,0:T(4,128)}, u32[]{:S(2)}) copy-start(f32[1,4,4,2048]{3,2,1,0:T(4,128)} %weight_ref.1) | copy-start | bytes 393220
  1.8 0.7 copy-start.2
  2.5 0.7 copy-start.3

commit v2 on v1

--- a/solution.py
+++ b/solution.py
@@ -70,10 +70,12 @@
     slopes_hbm,
     left_hbm,
     right_hbm,
+    foot_hbm,
+    weight_hbm,
+    fit_hbm,
+    out_ref,
     foot_ref,
     weight_ref,
-    fit_hbm,
-    out_ref,
     left,
     right,
     fit,
@@ -122,10 +124,14 @@
         return lax.rem(col + nc - j, nc)
 
     loads = [
-        pltpu.make_async_copy(right_hbm, right, load_sem.at[0]),
-        pltpu.make_async_copy(left_hbm, left, load_sem.at[1]),
+        pltpu.make_async_copy(foot_hbm, foot_ref, load_sem.at[0]),
+        pltpu.make_async_copy(weight_hbm, weight_ref, load_sem.at[1]),
         pltpu.make_async_copy(fit_hbm, fit, load_sem.at[2]),
+        pltpu.make_async_copy(right_hbm, right, load_sem.at[3]),
+        pltpu.make_async_copy(left_hbm, left, load_sem.at[4]),
     ]
+    for copy in loads:
+        copy.start()
 
     barrier = pltpu.get_barrier_semaphore()
     for j in range(1, nc):
@@ -164,13 +170,12 @@
         copy = pltpu.make_async_copy(
             slopes_hbm.at[pl.ds(start, share), pl.ds(b * tile, tile)],
             parts.at[col * slots + b],
-            load_sem.at[3 + b],
+            load_sem.at[5 + b],
         )
         copy.start()
         own.append(copy)
-    for copy in loads:
-        copy.start()
-    loads[2].wait()
+    for copy in loads[:3]:
+        copy.wait()
 
     layer_count, taps, pupil_count = foot_ref.shape[1:]
     points = mixing.shape[0]
@@ -197,7 +202,7 @@
         ).astype(jnp.bfloat16)
         return carry
 
-    cuts = [0, steps // 4, steps // 2, steps]
+    cuts = [0, steps // 4, steps // 2]
     lax.fori_loop(cuts[0], cuts[1], mix, 0)
 
     for copy in own:
@@ -249,8 +254,8 @@
     for j in range(nc):
         third[2 * j + 1].wait_recv()
         fourth[j].wait_recv()
-    loads[0].wait()
-    loads[1].wait()
+    loads[3].wait()
+    loads[4].wait()
 
     lane = lax.broadcasted_iota(jnp.int32, (1, rank_cols), 1)
     sums = []
@@ -275,46 +280,90 @@
             )
             copy.start()
             sums.append(copy)
-    lax.fori_loop(cuts[2], cuts[3], mix, 0)
-    for copy in sums:
-        copy.wait_recv()
+    marks = [steps * 2 // 3 + (steps - steps * 2 // 3) * n // rows_here for n in range(rows_here + 1)]
+    lax.fori_loop(cuts[2], marks[0], mix, 0)
+    relayed = []
+
+    def piece(r, b, i):
+        return layers.at[r, b, :, pl.ds(i * tile, tile)]
+
+    def pass_on(cond, r, b, i, send, recv, target):
+        copy = remote(piece(r, b, i), piece(r, b, i), send, recv, target)
+        if cond is None:
+            copy.start()
+        else:
+            pl.when(cond)(copy.start)
+        relayed.append((cond, copy))
+
+    def both(x, y):
+        return y if x is None else jnp.logical_and(x, y)
+
+    def hand_out(cond, s, up, i):
+        b = col - s if up else col + s
+        if s < nc - 1:
+            for way in (True, False) if s == 0 else (up,):
+                n = (s * 2 + way) * rows_here + i
+                more = both(cond, col < nc - 1 if way else col > 0)
+                target = {"col": lax.rem(col + (1 if way else nc - 1), nc)}
+                pass_on(more, here, b, i, z_send.at[n], z_recv.at[n], target)
+        n = (s * 2 + up) * rows_here + i
+        pass_on(cond, here, b, i, x_send.at[n], x_recv.at[n], across)
+        pass_on(cond, here, b, i, c_send.at[0, n], c_recv.at[0, n], sibling)
+
+    def await_recv(cond, r, b, i, send, recv):
+        copy = remote(piece(r, b, i), piece(r, b, i), send, recv, sibling)
+        if cond is None:
+            copy.wait_recv()
+        else:
+            pl.when(cond)(copy.wait_recv)
+
+    def valid(s, up):
+        return None if s == 0 else (col >= s if up else col < nc - s)
+
+    def take_z(s, up, i):
+        n = ((s - 1) * 2 + up) * rows_here + i
+        b = col - s if up else col + s
+        await_recv(valid(s, up), here, b, i, z_send.at[n], z_recv.at[n])
+        hand_out(valid(s, up), s, up, i)
+
+    def take_x(s, up, i):
+        n = (s * 2 + up) * rows_here + i
+        b = col - s if up else col + s
+        await_recv(valid(s, up), beside, b, i, x_send.at[n], x_recv.at[n])
+        pass_on(valid(s, up), beside, b, i, c_send.at[1, n], c_recv.at[1, n], sibling)
+
+    def ways(s):
+        return (True,) if s == 0 else (True, False)
+
     for i in range(rows_here):
+        for j in range(1, nc):
+            sums[i * (nc - 1) + j - 1].wait_recv()
         total = partial_sums[i, col].astype(jnp.float32)
         for j in range(1, nc):
             total += arrived[j - 1, i].astype(jnp.float32)
         layers[here, col, :, i * tile : (i + 1) * tile] = total.astype(jnp.bfloat16)
-
-    along = []
-    for j in range(1, nc):
-        at = layers.at[here, col]
-        copy = remote(at, at, z_send.at[j - 1], z_recv.at[j - 1], {"col": ahead(j)})
-        copy.start()
-        along.append(copy)
-    over, within = [], []
-
-    def spread_layers(j):
-        at = layers.at[here, behind(j)]
-        copy = remote(at, at, x_send.at[j], x_recv.at[j], across)
-        copy.start()
-        over.append(copy)
-        copy = remote(at, at, c_send.at[j], c_recv.at[j], sibling)
-        copy.start()
-        within.append(copy)
-
-    spread_layers(0)
-    for j in range(1, nc):
-        along[j - 1].wait_recv()
-        spread_layers(j)
-    passed = []
-    for j in range(nc):
-        over[j].wait_recv()
-        at = layers.at[beside, behind(j)]
-        copy = remote(at, at, c_send.at[nc + j], c_recv.at[nc + j], sibling)
-        copy.start()
-        passed.append(copy)
-    for j in range(nc):
-        within[j].wait_recv()
-        passed[j].wait_recv()
+        hand_out(None, 0, True, i)
+        if i < rows_here - 1:
+            lax.fori_loop(marks[i], marks[i + 1], mix, 0)
+    lax.fori_loop(marks[rows_here - 1], marks[rows_here], mix, 0)
+    for s in range(1, nc):
+        for i in range(rows_here):
+            for up in ways(s):
+                take_z(s, up, i)
+            for up in ways(s - 1):
+                take_x(s - 1, up, i)
+    for i in range(rows_here):
+        for up in ways(nc - 1):
+            take_x(nc - 1, up, i)
+    other = row * 2 + 1 - core
+    other_beside = (1 - row) * 2 + 1 - core
+    for s in range(nc):
+        for i in range(rows_here):
+            for up in ways(s):
+                n = (s * 2 + up) * rows_here + i
+                b = col - s if up else col + s
+                await_recv(valid(s, up), other, b, i, c_send.at[0, n], c_recv.at[0, n])
+                await_recv(valid(s, up), other_beside, b, i, c_send.at[1, n], c_recv.at[1, n])
     depth = layers.shape[3]
     total = jnp.zeros(out_ref.shape[1:], jnp.float32)
     for r in range(pieces):
@@ -324,8 +373,13 @@
             preferred_element_type=jnp.float32,
         )
     out_ref[0] = total.astype(jnp.bfloat16)
-    for copy in first + second + third + fourth + sums + along + over + within + passed:
+    for copy in first + second + third + fourth + sums:
         copy.wait_send()
+    for cond, copy in relayed:
+        if cond is None:
+            copy.wait_send()
+        else:
+            pl.when(cond)(copy.wait_send)
 
 
 def fused(
@@ -346,9 +400,11 @@
     return pl.pallas_call(
         functools.partial(fused_kernel, nc),
         out_shape=jax.ShapeDtypeStruct((1, frames, acts), bf16),
-        in_specs=[smem, smem, anywhere, anywhere, anywhere, vmem, vmem, anywhere],
+        in_specs=[smem, smem] + [anywhere] * 6,
         out_specs=vmem,
         scratch_shapes=[
+            pltpu.VMEM(footprint.shape, jnp.int32),
+            pltpu.VMEM(trace_weight.shape, jnp.float32),
             pltpu.VMEM(basis_left.shape, bf16),
             pltpu.VMEM(basis_right.shape, bf16),
             pltpu.VMEM(fitting.shape, bf16),
@@ -360,7 +416,7 @@
             pltpu.VMEM((rows_here, nc, frames // nc, tile), bf16),
             pltpu.VMEM((nc - 1, rows_here, frames // nc, tile), bf16),
             pltpu.VMEM((pieces, nc, frames // nc, rows_here * tile), bf16),
-            dma((3 + slots,)),
+            dma((5 + slots,)),
             dma(((nc - 1) * slots,)),
             dma(((nc - 1) * slots,)),
             dma((nc - 1,)),
@@ -371,12 +427,12 @@
             dma((2 * nc,)),
             dma(((nc - 1) * rows_here,)),
             dma(((nc - 1) * rows_here,)),
-            dma((nc - 1,)),
-            dma((nc - 1,)),
-            dma((nc,)),
-            dma((nc,)),
-            dma((2 * nc,)),
-            dma((2 * nc,)),
+            dma((2 * nc * rows_here,)),
+            dma((2 * nc * rows_here,)),
+            dma((2 * nc * rows_here,)),
+            dma((2 * nc * rows_here,)),
+            dma((2, 2 * nc * rows_here)),
+            dma((2, 2 * nc * rows_here)),
         ],
         compiler_params=pltpu.CompilerParams(
             collective_id=0, has_side_effects=True, vmem_limit_bytes=52 * 2**20

time: 79.8 us -> 74 us (0.927)
  the two profiles are of different devices: /device:TPU:27 before, /device:TPU:0 now
where the time goes in v2:
time: 74 us; the launch traced here: 73.4 us
  Pallas kernels  69.3 us (94%)
  local copies, waits for them, and re-layouts  4.12 us (6%)
    pallas_call x1, Pallas kernels, fused(): pl.pallas_call(functools.partial(fused_kernel, nc), out_shape=jax.ShapeDt...  69.3 us
    unnamed x9, local copies, waits for them, and re-layouts  4.12 us

profile of v2, /device:TPU:0, one launch (start us, length us, event | category | flops | bytes accessed | tf_op | source)
XLA Modules:
  0.0 73.4 jit_solution(5346340575317249302)
XLA Ops:
  0.0 0.0 copy-start
  0.0 0.9 %copy-done = s32[1,4,4,2048]{3,2,1,0:T(4,128)S(1)} copy-done((s32[1,4,4,2048]{3,2,1,0:T(4,128)S(1)}, s32[1,4,4,2048]{3,2,1,0:T(4,128)}, u32[]{:S(2)}) %copy-start) | copy-done | bytes 131096
  0.9 0.0 copy-start.1
  0.9 0.9 %copy-done.1 = f32[1,4,4,2048]{3,2,1,0:T(4,128)S(1)} copy-done((f32[1,4,4,2048]{3,2,1,0:T(4,128)S(1)}, f32[1,4,4,2048]{3,2,1,0:T(4,128)}, u32[]{:S(2)}) %copy-start.1) | copy-done | bytes 131096
  1.8 0.0 copy-start.2
  1.8 0.7 copy-done.2
  2.5 0.0 copy-start.3
  2.5 0.7 copy-done.3
  3.1 69.3 %shard_map.82 = bf16[1,512,1024]{2,1,0:T(8,128)(2,1)S(1)} custom-call(s32[16]{0:T(128)S(1)} %copy-done.3, s32[3,4]{1,0:T(4,128)S(1)} %copy-done.2, bf16[512,1024]{1,0:T(8,128)(2,1)} %slopes_hbm.1, bf16[3,4,256,256]{3,2,1,0:T(8,128)(2,1)} %left_hbm.1, bf16[3,4,256,256]{3,2,1,0:T(8,128)(2,1)} %right_hbm.1, s32[1,4,4,2048]{3,2,1,0:T(4,128)S(1)} %copy-done, ...), custom_call_target="tpu_custom_call" | custom-call | tf_op jit(solution)/shard_map/pallas_call | solution.py:400
  72.4 1.0 %copy.10 = bf16[1,512,1024]{2,1,0:T(8,128)(2,1)} copy(bf16[1,512,1024]{2,1,0:T(8,128)(2,1)S(1)} %shard_map.82) | data formatting | bytes 2097152
Async XLA Ops:
  0.0 0.9 %copy-start = (s32[1,4,4,2048]{3,2,1,0:T(4,128)S(1)}, s32[1,4,4,2048]{3,2,1,0:T(4,128)}, u32[]{:S(2)}) copy-start(s32[1,4,4,2048]{3,2,1,0:T(4,128)} %foot_hbm.1) | copy-start | bytes 393220
  0.9 0.9 %copy-start.1 = (f32[1,4,4,2048]{3,2,1,0:T(4,128)S(1)}, f32[1,4,4,2048]{3,2,1,0:T(4,128)}, u32[]{:S(2)}) copy-start(f32[1,4,4,2048]{3,2,1,0:T(4,128)} %weight_hbm.1) | copy-start | bytes 393220
  1.8 0.7 copy-start.2
  2.5 0.7 copy-start.3

commit v3 on v2

--- a/solution.py
+++ b/solution.py
@@ -79,7 +79,8 @@
     left,
     right,
     fit,
-    parts,
+    parts_a,
+    parts_b,
     picks,
     chosen,
     spread,
@@ -105,12 +106,14 @@
     c_send,
     c_recv,
 ):
+    parts = (parts_a, parts_b)
     rows_here, slots, tile, rank_cols = left.shape
     frames = slopes_hbm.shape[0]
-    quads = chosen.shape[0]
-    share = frames // quads
+    halves, quads = chosen.shape[:2]
+    part = frames // halves
+    share = part // quads
     pieces = quads // nc
-    block = frames // nc
+    block = part // nc
     col, row, core = lax.axis_index("col"), lax.axis_index("row"), lax.axis_index("dir")
     here = row * 2 + core
     beside = (1 - row) * 2 + core
@@ -150,30 +153,30 @@
             device_id_type=MESH,
         )
 
-    sent = []
-    for j in range(1, nc):
-        start = pl.multiple_of((ahead(j) * pieces + here) * share, share)
-        for b in range(slots):
-            copy = remote(
-                slopes_hbm.at[pl.ds(start, share), pl.ds(b * tile, tile)],
-                parts.at[col * slots + b],
-                a1_send.at[(j - 1) * slots + b],
-                a1_recv.at[(j - 1) * slots + b],
-                {"col": ahead(j)},
+    def mine(h, c, k):
+        start = pl.multiple_of(h * part + (c * pieces + here) * share, share)
+        return slopes_hbm.at[pl.ds(start, share), pl.ds(k * tile, tile)]
+
+    first = []
+    own = []
+    for h in range(halves):
+        for j in range(1, nc):
+            for k in range(slots):
+                copy = remote(
+                    mine(h, ahead(j), k),
+                    parts[h].at[col * slots + k],
+                    a1_send.at[h, (j - 1) * slots + k],
+                    a1_recv.at[h, (j - 1) * slots + k],
+                    {"col": ahead(j)},
+                )
+                copy.start()
+                first.append(copy)
+        for k in range(slots):
+            copy = pltpu.make_async_copy(
+                mine(h, col, k), parts[h].at[col * slots + k], load_sem.at[5 + h * slots + k]
             )
             copy.start()
-            sent.append(copy)
-    first = sent
-    start = pl.multiple_of((col * pieces + here) * share, share)
-    own = []
-    for b in range(slots):
-        copy = pltpu.make_async_copy(
-            slopes_hbm.at[pl.ds(start, share), pl.ds(b * tile, tile)],
-            parts.at[col * slots + b],
-            load_sem.at[5 + b],
-        )
-        copy.start()
-        own.append(copy)
+            own.append(copy)
     for copy in loads[:3]:
         copy.wait()
 
@@ -202,90 +205,101 @@
         ).astype(jnp.bfloat16)
         return carry
 
-    cuts = [0, steps // 4, steps // 2]
-    lax.fori_loop(cuts[0], cuts[1], mix, 0)
-
-    for copy in own:
-        copy.wait()
-    for copy in first:
-        copy.wait_recv()
+    cuts = [steps * n // 12 for n in (0, 3, 5, 9, 11, 12)]
+
+    def mix_part(n):
+        lax.fori_loop(cuts[n], cuts[n + 1], mix, 0)
+
+    mix_part(0)
+
     second = []
-    for j in range(nc):
-        for k in range(slots):
-            picks[ahead(j), k] = parts[owner_ref[ahead(j) * slots + k]]
-        if j:
-            copy = remote(
-                picks.at[ahead(j)],
-                chosen.at[col * pieces + here],
-                a2_send.at[j - 1],
-                a2_recv.at[j - 1],
-                {"col": ahead(j)},
-            )
-            copy.start()
-            second.append(copy)
-    chosen[col * pieces + here] = picks[col]
-
-    third = []
-
-    def spread_share(j):
-        at = behind(j) * pieces + here
+    for h in range(halves):
+        for copy in own[h * slots : (h + 1) * slots]:
+            copy.wait()
+        for copy in first[h * (nc - 1) * slots : (h + 1) * (nc - 1) * slots]:
+            copy.wait_recv()
+        for j in list(range(1, nc)) + [0]:
+            for k in range(slots):
+                picks[h, ahead(j), k] = parts[h][owner_ref[ahead(j) * slots + k]]
+            if j:
+                copy = remote(
+                    picks.at[h, ahead(j)],
+                    chosen.at[h, col * pieces + here],
+                    a2_send.at[h, j - 1],
+                    a2_recv.at[h, j - 1],
+                    {"col": ahead(j)},
+                )
+                copy.start()
+                second.append(copy)
+        chosen[h, col * pieces + here] = picks[h, col]
+
+    third, fourth = [], []
+
+    def spread_share(h, j):
+        at = chosen.at[h, behind(j) * pieces + here]
         for send, recv, target in (
-            (a3x_send.at[j], a3x_recv.at[j], across),
-            (a3c_send.at[j], a3c_recv.at[j], sibling),
+            (a3x_send.at[h, j], a3x_recv.at[h, j], across),
+            (a3c_send.at[h, j], a3c_recv.at[h, j], sibling),
         ):
-            copy = remote(chosen.at[at], chosen.at[at], send, recv, target)
+            copy = remote(at, at, send, recv, target)
             copy.start()
             third.append(copy)
 
-    spread_share(0)
-    lax.fori_loop(cuts[1], cuts[2], mix, 0)
-    for j in range(1, nc):
-        second[j - 1].wait_recv()
-        spread_share(j)
-    fourth = []
-    for j in range(nc):
-        third[2 * j].wait_recv()
-        at = behind(j) * pieces + beside
-        copy = remote(
-            chosen.at[at], chosen.at[at], a3c_send.at[nc + j], a3c_recv.at[nc + j], sibling
-        )
+    def forward_share(h, j):
+        third[2 * (h * nc + j)].wait_recv()
+        at = chosen.at[h, behind(j) * pieces + beside]
+        copy = remote(at, at, a3c_send.at[h, nc + j], a3c_recv.at[h, nc + j], sibling)
         copy.start()
         fourth.append(copy)
-    for j in range(nc):
-        third[2 * j + 1].wait_recv()
-        fourth[j].wait_recv()
+
+    mix_part(1)
+    for h in range(halves):
+        spread_share(h, 0)
+        for j in range(1, nc):
+            second[h * (nc - 1) + j - 1].wait_recv()
+            spread_share(h, j)
     loads[3].wait()
     loads[4].wait()
 
     lane = lax.broadcasted_iota(jnp.int32, (1, rank_cols), 1)
     sums = []
-    for i in range(rows_here):
-        total = jnp.zeros((frames, tile), jnp.float32)
-        for k in range(slots):
-            coeffs = jnp.dot(
-                chosen[:, k].reshape(frames, tile), right[i, k], preferred_element_type=jnp.float32
+    for h in range(halves):
+        for j in range(nc):
+            forward_share(h, j)
+        for j in range(nc):
+            third[2 * (h * nc + j) + 1].wait_recv()
+            fourth[h * nc + j].wait_recv()
+        for i in range(rows_here):
+            total = jnp.zeros((part, tile), jnp.float32)
+            for k in range(slots):
+                coeffs = jnp.dot(
+                    chosen[h, :, k].reshape(part, tile),
+                    right[i, k],
+                    preferred_element_type=jnp.float32,
+                )
+                coeffs = jnp.where(lane < ranks_ref[i, k] * RB, coeffs, 0.0).astype(jnp.bfloat16)
+                total += lax.dot_general(
+                    coeffs, left[i, k], (((1,), (1,)), ((), ())), preferred_element_type=jnp.float32
+                )
+            partial_sums[h, :, :, i * tile : (i + 1) * tile] = total.astype(jnp.bfloat16).reshape(
+                nc, block, tile
             )
-            coeffs = jnp.where(lane < ranks_ref[i, k] * RB, coeffs, 0.0).astype(jnp.bfloat16)
-            total += lax.dot_general(
-                coeffs, left[i, k], (((1,), (1,)), ((), ())), preferred_element_type=jnp.float32
-            )
-        partial_sums[i] = total.astype(jnp.bfloat16).reshape(nc, block, tile)
         for j in range(1, nc):
             copy = remote(
-                partial_sums.at[i, ahead(j)],
-                arrived.at[j - 1, i],
-                rs_send.at[(j - 1) * rows_here + i],
-                rs_recv.at[(j - 1) * rows_here + i],
+                partial_sums.at[h, ahead(j)],
+                arrived.at[h, j - 1],
+                rs_send.at[h, j - 1],
+                rs_recv.at[h, j - 1],
                 {"col": ahead(j)},
             )
             copy.start()
             sums.append(copy)
-    marks = [steps * 2 // 3 + (steps - steps * 2 // 3) * n // rows_here for n in range(rows_here + 1)]
-    lax.fori_loop(cuts[2], marks[0], mix, 0)
+    mix_part(2)
+
     relayed = []
 
     def piece(r, b, i):
-        return layers.at[r, b, :, pl.ds(i * tile, tile)]
+        return layers.at[r, i, b]
 
     def pass_on(cond, r, b, i, send, recv, target):
         copy = remote(piece(r, b, i), piece(r, b, i), send, recv, target)
@@ -302,11 +316,11 @@
         b = col - s if up else col + s
         if s < nc - 1:
             for way in (True, False) if s == 0 else (up,):
-                n = (s * 2 + way) * rows_here + i
+                n = (s * 2 + way) * halves + i
                 more = both(cond, col < nc - 1 if way else col > 0)
                 target = {"col": lax.rem(col + (1 if way else nc - 1), nc)}
                 pass_on(more, here, b, i, z_send.at[n], z_recv.at[n], target)
-        n = (s * 2 + up) * rows_here + i
+        n = (s * 2 + up) * halves + i
         pass_on(cond, here, b, i, x_send.at[n], x_recv.at[n], across)
         pass_on(cond, here, b, i, c_send.at[0, n], c_recv.at[0, n], sibling)
 
@@ -321,13 +335,13 @@
         return None if s == 0 else (col >= s if up else col < nc - s)
 
     def take_z(s, up, i):
-        n = ((s - 1) * 2 + up) * rows_here + i
+        n = ((s - 1) * 2 + up) * halves + i
         b = col - s if up else col + s
         await_recv(valid(s, up), here, b, i, z_send.at[n], z_recv.at[n])
         hand_out(valid(s, up), s, up, i)
 
     def take_x(s, up, i):
-        n = (s * 2 + up) * rows_here + i
+        n = (s * 2 + up) * halves + i
         b = col - s if up else col + s
         await_recv(valid(s, up), beside, b, i, x_send.at[n], x_recv.at[n])
         pass_on(valid(s, up), beside, b, i, c_send.at[1, n], c_recv.at[1, n], sibling)
@@ -335,44 +349,41 @@
     def ways(s):
         return (True,) if s == 0 else (True, False)
 
-    for i in range(rows_here):
+    for h in range(halves):
         for j in range(1, nc):
-            sums[i * (nc - 1) + j - 1].wait_recv()
-        total = partial_sums[i, col].astype(jnp.float32)
+            sums[h * (nc - 1) + j - 1].wait_recv()
+        total = partial_sums[h, col].astype(jnp.float32)
         for j in range(1, nc):
-            total += arrived[j - 1, i].astype(jnp.float32)
-        layers[here, col, :, i * tile : (i + 1) * tile] = total.astype(jnp.bfloat16)
-        hand_out(None, 0, True, i)
-        if i < rows_here - 1:
-            lax.fori_loop(marks[i], marks[i + 1], mix, 0)
-    lax.fori_loop(marks[rows_here - 1], marks[rows_here], mix, 0)
+            total += arrived[h, j - 1].astype(jnp.float32)
+        layers[here, h, col] = total.astype(jnp.bfloat16)
+        hand_out(None, 0, True, h)
+        mix_part(3 + (h == halves - 1))
     for s in range(1, nc):
-        for i in range(rows_here):
+        for h in range(halves):
             for up in ways(s):
-                take_z(s, up, i)
+                take_z(s, up, h)
             for up in ways(s - 1):
-                take_x(s - 1, up, i)
-    for i in range(rows_here):
-        for up in ways(nc - 1):
-            take_x(nc - 1, up, i)
+                take_x(s - 1, up, h)
     other = row * 2 + 1 - core
     other_beside = (1 - row) * 2 + 1 - core
-    for s in range(nc):
-        for i in range(rows_here):
+    depth = layers.shape[4]
+    for h in range(halves):
+        for up in ways(nc - 1):
+            take_x(nc - 1, up, h)
+        for s in range(nc):
             for up in ways(s):
-                n = (s * 2 + up) * rows_here + i
+                n = (s * 2 + up) * halves + h
                 b = col - s if up else col + s
-                await_recv(valid(s, up), other, b, i, c_send.at[0, n], c_recv.at[0, n])
-                await_recv(valid(s, up), other_beside, b, i, c_send.at[1, n], c_recv.at[1, n])
-    depth = layers.shape[3]
-    total = jnp.zeros(out_ref.shape[1:], jnp.float32)
-    for r in range(pieces):
-        total += jnp.dot(
-            layers[r].reshape(frames, depth),
-            mixing[r * depth : (r + 1) * depth, :],
-            preferred_element_type=jnp.float32,
-        )
-    out_ref[0] = total.astype(jnp.bfloat16)
+                await_recv(valid(s, up), other, b, h, c_send.at[0, n], c_recv.at[0, n])
+                await_recv(valid(s, up), other_beside, b, h, c_send.at[1, n], c_recv.at[1, n])
+        total = jnp.zeros((part, out_ref.shape[2]), jnp.float32)
+        for r in range(pieces):
+            total += jnp.dot(
+                layers[r, h].reshape(part, depth),
+                mixing[r * depth : (r + 1) * depth, :],
+                preferred_element_type=jnp.float32,
+            )
+        out_ref[0, h * part : (h + 1) * part, :] = total.astype(jnp.bfloat16)
     for copy in first + second + third + fourth + sums:
         copy.wait_send()
     for cond, copy in relayed:
@@ -388,7 +399,9 @@
     frames = slopes_in.shape[0]
     rows_here, slots, tile, rank_cols = basis_left.shape
     pieces = 4
-    share = frames // (nc * pieces)
+    halves = 2
+    part = frames // halves
+    share = part // (nc * pieces)
     points = rows_here * tile * pieces
     pupil_count, acts = fitting.shape
     step = tile
@@ -409,30 +422,31 @@
             pltpu.VMEM(basis_right.shape, bf16),
             pltpu.VMEM(fitting.shape, bf16),
             pltpu.VMEM((nc * slots, share, tile), bf16),
-            pltpu.VMEM((nc, slots, share, tile), bf16),
-            pltpu.VMEM((nc * pieces, slots, share, tile), bf16),
+            pltpu.VMEM((nc * slots, share, tile), bf16),
+            pltpu.VMEM((halves, nc, slots, share, tile), bf16),
+            pltpu.VMEM((halves, nc * pieces, slots, share, tile), bf16),
             pltpu.VMEM((step, pupil_count), bf16),
             pltpu.VMEM((points, acts), bf16),
-            pltpu.VMEM((rows_here, nc, frames // nc, tile), bf16),
-            pltpu.VMEM((nc - 1, rows_here, frames // nc, tile), bf16),
-            pltpu.VMEM((pieces, nc, frames // nc, rows_here * tile), bf16),
-            dma((5 + slots,)),
-            dma(((nc - 1) * slots,)),
-            dma(((nc - 1) * slots,)),
-            dma((nc - 1,)),
-            dma((nc - 1,)),
-            dma((nc,)),
-            dma((nc,)),
-            dma((2 * nc,)),
-            dma((2 * nc,)),
-            dma(((nc - 1) * rows_here,)),
-            dma(((nc - 1) * rows_here,)),
-            dma((2 * nc * rows_here,)),
-            dma((2 * nc * rows_here,)),
-            dma((2 * nc * rows_here,)),
-            dma((2 * nc * rows_here,)),
-            dma((2, 2 * nc * rows_here)),
-            dma((2, 2 * nc * rows_here)),
+            pltpu.VMEM((halves, nc, part // nc, rows_here * tile), bf16),
+            pltpu.VMEM((halves, nc - 1, part // nc, rows_here * tile), bf16),
+            pltpu.VMEM((pieces, halves, nc, part // nc, rows_here * tile), bf16),
+            dma((5 + halves * slots,)),
+            dma((halves, (nc - 1) * slots)),
+            dma((halves, (nc - 1) * slots)),
+            dma((halves, nc - 1)),
+            dma((halves, nc - 1)),
+            dma((halves, nc)),
+            dma((halves, nc)),
+            dma((halves, 2 * nc)),
+            dma((halves, 2 * nc)),
+            dma((halves, nc - 1)),
+            dma((halves, nc - 1)),
+            dma((2 * nc * halves,)),
+            dma((2 * nc * halves,)),
+            dma((2 * nc * halves,)),
+            dma((2 * nc * halves,)),
+            dma((2, 2 * nc * halves)),
+            dma((2, 2 * nc * halves)),
         ],
         compiler_params=pltpu.CompilerParams(
             collective_id=0, has_side_effects=True, vmem_limit_bytes=52 * 2**20
@@ -470,7 +484,7 @@
             mesh.shape["row"] == 2
             and mesh.shape["dir"] == 2
             and nc > 1
-            and slopes_in.shape[0] % (nc * pieces * 16) == 0
+            and slopes_in.shape[0] % (2 * nc * pieces * 16) == 0
             and slopes_in.shape[1] == basis_left.shape[1] * tile
             and per_layer % tile == 0
         )

time: 74 us -> 68.9 us (0.931)
  Pallas kernels: 69.3 us -> 64.6 us
    pallas_call x1, Pallas kernels: 69.3 us -> 64.6 us  [fused(): pl.pallas_call(functools.partial(fused_kernel, nc), out_shape=jax.ShapeDt...]
where the time goes in v3:
time: 68.9 us; the launch traced here: 68.8 us
  Pallas kernels  64.6 us (94%)
  local copies, waits for them, and re-layouts  4.12 us (6%)
    pallas_call x1, Pallas kernels, fused(): pl.pallas_call(functools.partial(fused_kernel, nc), out_shape=jax.ShapeDt...  64.6 us
    unnamed x9, local copies, waits for them, and re-layouts  4.12 us

profile of v3, /device:TPU:0, one launch (start us, length us, event | category | flops | bytes accessed | tf_op | source)
XLA Modules:
  0.0 68.8 jit_solution(9267596929228734278)
XLA Ops:
  0.0 0.0 copy-start
  0.0 0.9 %copy-done = s32[1,4,4,2048]{3,2,1,0:T(4,128)S(1)} copy-done((s32[1,4,4,2048]{3,2,1,0:T(4,128)S(1)}, s32[1,4,4,2048]{3,2,1,0:T(4,128)}, u32[]{:S(2)}) %copy-start) | copy-done | bytes 131096
  0.9 0.0 copy-start.1
  0.9 0.9 %copy-done.1 = f32[1,4,4,2048]{3,2,1,0:T(4,128)S(1)} copy-done((f32[1,4,4,2048]{3,2,1,0:T(4,128)S(1)}, f32[1,4,4,2048]{3,2,1,0:T(4,128)}, u32[]{:S(2)}) %copy-start.1) | copy-done | bytes 131096
  1.8 0.0 copy-start.2
  1.8 0.7 copy-done.2
  2.5 0.0 copy-start.3
  2.5 0.7 copy-done.3
  3.1 64.6 %shard_map.82 = bf16[1,512,1024]{2,1,0:T(8,128)(2,1)S(1)} custom-call(s32[16]{0:T(128)S(1)} %copy-done.3, s32[3,4]{1,0:T(4,128)S(1)} %copy-done.2, bf16[512,1024]{1,0:T(8,128)(2,1)} %slopes_hbm.1, bf16[3,4,256,256]{3,2,1,0:T(8,128)(2,1)} %left_hbm.1, bf16[3,4,256,256]{3,2,1,0:T(8,128)(2,1)} %right_hbm.1, s32[1,4,4,2048]{3,2,1,0:T(4,128)S(1)} %copy-done, ...), custom_call_target="tpu_custom_call" | custom-call | tf_op jit(solution)/shard_map/pallas_call | solution.py:413
  67.8 1.0 %copy.10 = bf16[1,512,1024]{2,1,0:T(8,128)(2,1)} copy(bf16[1,512,1024]{2,1,0:T(8,128)(2,1)S(1)} %shard_map.82) | data formatting | bytes 2097152
Async XLA Ops:
  0.0 0.9 %copy-start = (s32[1,4,4,2048]{3,2,1,0:T(4,128)S(1)}, s32[1,4,4,2048]{3,2,1,0:T(4,128)}, u32[]{:S(2)}) copy-start(s32[1,4,4,2048]{3,2,1,0:T(4,128)} %foot_hbm.1) | copy-start | bytes 393220
  0.9 0.9 %copy-start.1 = (f32[1,4,4,2048]{3,2,1,0:T(4,128)S(1)}, f32[1,4,4,2048]{3,2,1,0:T(4,128)}, u32[]{:S(2)}) copy-start(f32[1,4,4,2048]{3,2,1,0:T(4,128)} %weight_hbm.1) | copy-start | bytes 393220
  1.8 0.7 copy-start.2
  2.5 0.7 copy-start.3
